TPU v7x, 32 devices: a whole 2x2x4 slice. The times are simulated.
32 devices in a mesh: dp: 4 (over z), mp: 8 (over y, x, core).
Axes of the slice: x: 2, y: 2, z: 4, core: 2. Of those that a mesh axis runs over, the one named last changes fastest.
Arguments:
- guess_vectors: bfloat16 [128, 16, 4096], P(('dp', 'mp')), may hold values from -6 to 6
- preceding_symbol_vector: bfloat16 [128, 4096], P(('dp', 'mp')), may hold values from -6 to 6
- earlier_memory_matrix: float32 [128, 64, 64, 64], P('dp', 'mp'), may hold values from -4 to 4
- lag_blend_factor: float32 [4096], replicated, may hold values from 0 to 1
- constant_lag_blends: float32 [5, 4096], replicated, may hold values from 0 to 1
- blending_lower_matrix: bfloat16 [4096, 160], replicated, may hold values from -0.09375 to 0.09375
- blending_raise_matrix: bfloat16 [5, 32, 4096], replicated, may hold values from -1 to 1
- constant_fading: float32 [4096], P('mp'), may hold values from -6 to -1
- fading_lower_matrix: bfloat16 [4096, 64], replicated, may hold values from -0.09375 to 0.09375
- fading_raise_matrix: bfloat16 [64, 4096], P(None, 'mp'), may hold values from -1 to 1
- diagonal_boost: float32 [64, 64], P('mp'), may hold values from -3 to 3
- acceptor_matrix: bfloat16 [4096, 4096], P('dp', 'mp'), may hold values from -0.09375 to 0.09375
- lookup_matrix: bfloat16 [4096, 4096], P('dp', 'mp'), may hold values from -0.09375 to 0.09375
- payload_matrix: bfloat16 [4096, 4096], P('dp', 'mp'), may hold values from -0.09375 to 0.09375
- gating_matrix: bfloat16 [4096, 4096], P('dp', 'mp'), may hold values from -0.09375 to 0.09375
- emission_matrix: bfloat16 [4096, 4096], P('mp', 'dp'), may hold values from -0.09375 to 0.09375
- groupwise_scaling_factor: float32 [4096], P('mp'), may hold values from 0.1 to 1.9
- groupwise_scaling_offset: float32 [4096], P('mp'), may hold values from -3 to 3
- usable_guess_amount: int32 [128], replicated, may hold values from 1 to 16, as said below
- approved_guesses: int32 [128], replicated, may hold values from 0 to 16, as said below
- destination_slot: int32 [128], replicated, may hold values from 0 to 127, as said below
Outputs:
- layer_out: bfloat16 [128, 16, 4096], P(('dp', 'mp'))
- next_state: float32 [128, 64, 64, 64], P('dp', 'mp')
- next_edge: bfloat16 [128, 4096], P('dp', 'mp')
Inputs may be any that keep to these rules, and one draw needn't show every extreme that they name: `usable_guess_amount`: some request has all 16 draft tokens valid. approved_guesses[b] <= usable_guess_amount[b]; some request accepts all 16. destination_slot is a permutation of the requests. Of the 32 requests of one aligned block, at most 16 have owner slots in one aligned block of 32 slots, and some pair of blocks reaches 16.
All inputs are finite; a program needn't handle non-finite values.
Results may differ from a plain program's by a relative error of at most 0.007.
Values may be sent and summed in bfloat16 or wider, within the bound.
A program may use at most 256 MiB of HBM per device.

v0:
```python
import jax
import jax.numpy as jnp
from jax import lax
from jax.sharding import PartitionSpec as P

GROUP_DIMENSION = 64
norm_eps = 0.00064


def token_mixes(
    guess_vectors,
    edges,
    lag_blend_factor,
    constant_lag_blends,
    blending_lower_matrix,
    blending_raise_matrix,
):
    previous = jnp.concatenate([edges[:, None, :], guess_vectors[:, :-1, :]], axis=1)
    width = guess_vectors.shape[-1]
    current_input = guess_vectors.reshape(-1, width).astype(jnp.float32)
    shift_difference = previous.reshape(-1, width).astype(jnp.float32) - current_input
    shift_blended = (current_input + shift_difference * lag_blend_factor).astype(jnp.bfloat16)
    mixing_inner_all = jnp.tanh(
        jnp.dot(shift_blended, blending_lower_matrix, preferred_element_type=jnp.float32)
    ).astype(jnp.bfloat16)
    mixing_inner_width = blending_raise_matrix.shape[1]
    shift_mixed_rows = []
    for mix_component in range(5):
        mixing_inner_part = jnp.dot(
            mixing_inner_all[
                :, mix_component * mixing_inner_width : (mix_component + 1) * mixing_inner_width
            ],
            blending_raise_matrix[mix_component],
            preferred_element_type=jnp.float32,
        )
        shift_mixed_rows.append(
            (
                current_input
                + shift_difference * (constant_lag_blends[mix_component] + mixing_inner_part)
            ).astype(jnp.bfloat16)
        )
    return shift_mixed_rows


def wkv_blocks(
    acceptor_vectors,
    lookup_vectors,
    payload_vectors,
    logarithmic_fading_entries,
    diagonal_boost,
    starting_memory,
    approved_guesses,
):
    draft = acceptor_vectors.shape[1]
    cumulative = jnp.cumsum(logarithmic_fading_entries, axis=1)
    starts = jnp.concatenate(
        [jnp.zeros_like(logarithmic_fading_entries[:, :1]), cumulative], axis=1
    )
    before = starts[:, :draft]
    from_start = jnp.einsum(
        "bthi,bhij->bthj",
        acceptor_vectors * jnp.exp(before),
        starting_memory,
        precision=lax.Precision.HIGHEST,
    )
    later = jnp.arange(draft)[:, None] > jnp.arange(draft)[None, :]
    exponent = before[:, :, None] - cumulative[:, None, :]
    exponent = jnp.where(later[None, :, :, None, None], exponent, -1e30)
    scores = jnp.sum(
        acceptor_vectors[:, :, None] * lookup_vectors[:, None, :] * jnp.exp(exponent), axis=-1
    )
    inner = jnp.einsum("btsh,bshj->bthj", scores, payload_vectors, precision=lax.Precision.HIGHEST)
    diagonal_boost_contribution = (
        jnp.sum(acceptor_vectors * diagonal_boost * lookup_vectors, axis=-1, keepdims=True)
        * payload_vectors
    )
    outputs = from_start + inner + diagonal_boost_contribution
    at_accept = jnp.take_along_axis(starts, approved_guesses[:, None, None, None], axis=1)[:, 0]
    used = jnp.arange(draft)[None, :] < approved_guesses[:, None]
    coef_exp = jnp.where(used[:, :, None, None], at_accept[:, None] - cumulative, -1e30)
    weighted = jnp.exp(coef_exp) * lookup_vectors
    picked = jnp.exp(at_accept)[..., None] * starting_memory + jnp.einsum(
        "bshi,bshj->bhij", weighted, payload_vectors, precision=lax.Precision.HIGHEST
    )
    return (outputs, picked)


def gated_norm(outputs, gate_raw, gain, bias):
    centre = jnp.mean(outputs, axis=-1, keepdims=True)
    spread = outputs - centre
    variance = jnp.mean(spread * spread, axis=-1, keepdims=True)
    normed = (spread * lax.rsqrt(variance + norm_eps)).reshape(outputs.shape[0], -1)
    return ((normed * gain + bias) * jax.nn.silu(gate_raw)).astype(jnp.bfloat16)


def on_device(
    guess_vectors,
    preceding_symbol_vector,
    earlier_memory_matrix,
    lag_blend_factor,
    constant_lag_blends,
    blending_lower_matrix,
    blending_raise_matrix,
    constant_fading,
    fading_lower_matrix,
    fading_raise_matrix,
    diagonal_boost,
    acceptor_matrix,
    lookup_matrix,
    payload_matrix,
    gating_matrix,
    emission_matrix,
    groupwise_scaling_factor,
    groupwise_scaling_offset,
    usable_guess_amount,
    approved_guesses,
    destination_slot,
):
    own_reqs, draft, width = guess_vectors.shape
    group_count = lax.axis_size("mp")
    row_groups = lax.axis_size("dp")
    row_reqs = own_reqs * group_count
    row_index = lax.axis_index("dp")
    group_index = lax.axis_index("mp")
    local_width = acceptor_matrix.shape[1]
    local_heads = local_width // GROUP_DIMENSION
    gathered, edges_all = (
        lax.all_gather(guess_vectors, "mp", axis=0, tiled=True),
        lax.all_gather(preceding_symbol_vector, "mp", axis=0, tiled=True),
    )
    shift_mixed_rows = token_mixes(
        gathered,
        edges_all,
        lag_blend_factor,
        constant_lag_blends,
        blending_lower_matrix,
        blending_raise_matrix,
    )
    token_rows = row_reqs * draft
    sources = (shift_mixed_rows[3], shift_mixed_rows[1], shift_mixed_rows[2], shift_mixed_rows[4])
    pieces = (
        lax.all_gather(acceptor_matrix, "dp", axis=0, tiled=True),
        lax.all_gather(lookup_matrix, "dp", axis=0, tiled=True),
        lax.all_gather(payload_matrix, "dp", axis=0, tiled=True),
        lax.all_gather(gating_matrix, "dp", axis=0, tiled=True),
    )
    acceptor_vectors, lookup_vectors, payload_vectors, gate_raw = tuple(
        (
            jnp.dot(source_rows, piece, preferred_element_type=jnp.float32)
            for source_rows, piece in zip(sources, pieces)
        )
    )
    decay_inner_rows = jnp.tanh(
        jnp.dot(shift_mixed_rows[0], fading_lower_matrix, preferred_element_type=jnp.float32)
    ).astype(jnp.bfloat16)
    logarithmic_fading_entries = -jnp.exp(
        constant_fading
        + jnp.dot(decay_inner_rows, fading_raise_matrix, preferred_element_type=jnp.float32)
    )

    def to_heads(values):
        return values.reshape(row_reqs, draft, local_heads, GROUP_DIMENSION)

    row_accepted = lax.dynamic_slice_in_dim(approved_guesses, row_index * row_reqs, row_reqs)
    outputs, picked = wkv_blocks(
        to_heads(acceptor_vectors),
        to_heads(lookup_vectors),
        to_heads(payload_vectors),
        to_heads(logarithmic_fading_entries),
        diagonal_boost,
        earlier_memory_matrix,
        row_accepted,
    )
    hidden = gated_norm(
        outputs.reshape(token_rows, local_heads, GROUP_DIMENSION),
        gate_raw,
        groupwise_scaling_factor,
        groupwise_scaling_offset,
    )
    out_cols = lax.all_gather(emission_matrix, "dp", axis=1, tiled=True)
    attended = lax.psum_scatter(
        jnp.dot(hidden, out_cols, preferred_element_type=jnp.float32).astype(jnp.bfloat16),
        "mp",
        scatter_dimension=0,
        tiled=True,
    ).astype(jnp.float32)
    own_start = (row_index * group_count + group_index) * own_reqs
    own_lengths = lax.dynamic_slice_in_dim(usable_guess_amount, own_start, own_reqs)
    valid_mask = jnp.arange(draft, dtype=jnp.int32)[None, :] < own_lengths[:, None]
    layer_out = (
        guess_vectors.astype(jnp.float32)
        + jnp.where(
            valid_mask[..., None],
            attended.reshape(own_reqs, draft, width),
            jnp.zeros((), jnp.float32),
        )
    ).astype(jnp.bfloat16)
    edge_rows = jnp.concatenate([edges_all[:, None, :], gathered], axis=1)
    edge_cols = lax.dynamic_slice_in_dim(edge_rows, group_index * local_width, local_width, 2)
    chosen = jnp.take_along_axis(edge_cols, row_accepted[:, None, None], axis=1)[:, 0]
    capacity = 2 * row_reqs // row_groups
    target_rows = (destination_slot // row_reqs).reshape(row_groups, row_reqs)
    onehot = (
        target_rows[:, :, None] == jnp.arange(row_groups, dtype=jnp.int32)[None, None, :]
    ).astype(jnp.int32)
    earlier = jnp.cumsum(onehot, axis=1) - onehot
    ranks = jnp.sum(earlier * onehot, axis=-1)
    my_targets = lax.dynamic_index_in_dim(target_rows, row_index, 0, keepdims=False)
    my_ranks = lax.dynamic_index_in_dim(ranks, row_index, 0, keepdims=False)
    selected = (
        my_targets[:, None, None] == jnp.arange(row_groups, dtype=jnp.int32)[None, :, None]
    ) & (my_ranks[:, None, None] == jnp.arange(capacity, dtype=jnp.int32)[None, None, :])
    source_index = jnp.sum(
        selected.astype(jnp.int32) * jnp.arange(row_reqs, dtype=jnp.int32)[:, None, None], axis=0
    )
    filled = jnp.any(selected, axis=0)
    send_state = jnp.where(
        filled[..., None, None, None], picked[source_index], jnp.zeros((), jnp.float32)
    )
    send_edge = jnp.where(
        filled[..., None], chosen[source_index].astype(jnp.float32), jnp.zeros((), jnp.float32)
    )
    recv_state, recv_edge = (
        lax.all_to_all(
            send_state.astype(jnp.bfloat16), "dp", split_axis=0, concat_axis=0, tiled=True
        ).astype(send_state.dtype),
        lax.all_to_all(
            send_edge.astype(jnp.bfloat16), "dp", split_axis=0, concat_axis=0, tiled=True
        ).astype(send_edge.dtype),
    )
    wanted = row_index * row_reqs + jnp.arange(row_reqs, dtype=jnp.int32)
    total_reqs = destination_slot.shape[0]
    matches = (destination_slot[None, :] == wanted[:, None]).astype(jnp.int32)
    which = jnp.sum(matches * jnp.arange(total_reqs, dtype=jnp.int32)[None, :], axis=1)
    flat_index = which // row_reqs * capacity + ranks.reshape(-1)[which]
    next_state = recv_state.reshape(
        row_groups * capacity, local_heads, GROUP_DIMENSION, GROUP_DIMENSION
    )[flat_index]
    next_edge = recv_edge.reshape(row_groups * capacity, local_width)[flat_index].astype(
        jnp.bfloat16
    )
    return (layer_out, next_state, next_edge)


def solution(mesh):
    in_specs = (
        P(("dp", "mp"), None, None),
        P(("dp", "mp"), None),
        P("dp", "mp", None, None),
        P(),
        P(),
        P(),
        P(),
        P("mp"),
        P(),
        P(None, "mp"),
        P("mp", None),
        P("dp", "mp"),
        P("dp", "mp"),
        P("dp", "mp"),
        P("dp", "mp"),
        P("mp", "dp"),
        P("mp"),
        P("mp"),
        P(),
        P(),
        P(),
    )
    out_specs = (P(("dp", "mp"), None, None), P("dp", "mp", None, None), P("dp", "mp"))
    return jax.shard_map(
        on_device, mesh=mesh, in_specs=in_specs, out_specs=out_specs, check_vma=False
    )
```

profile of v0, /device:TPU:0, one launch (start us, length us, event | category | flops | bytes accessed | tf_op | source)
XLA Modules:
  0.0 585.9 jit_solution(18396825524794450216)
XLA Ops:
  12.2 10.8 %all-gather = bf16[8,4,4096]{2,1,0:T(4,128)(2,1)S(1)} all-gather(bf16[1,4,4096]{2,1,0:T(4,128)(2,1)S(1)} %bitcast.122), channel_id=1, replica_groups=mesh['dp'=4,'mp'=8] {'mp'}, dimensions={0}, use_global_device_ids=true | all-gather | bytes 294912 | tf_op jit(solution)/shard_map/all_gather | solution.py:129
  23.9 25.6 %all-gather.8.cloned.1.call-done = bf16[32,16,4096]{2,1,0:T(8,128)(2,1)} async-done(((bf16[4,16,4096]{2,1,0:T(8,128)(2,1)}), bf16[32,16,4096]{2,1,0:T(8,128)(2,1)}) %all-gather.8.cloned.1.call-update) | async-done | bytes 4194320 | tf_op jit(solution)/shard_map/all_gather | solution.py:128
  49.4 3.7 pad_maximum_fusion
  57.1 74.7 %all-gather.12.cloned.1.call-done = bf16[4096,512]{1,0:T(8,128)(2,1)} async-done(((bf16[1024,512]{1,0:T(8,128)(2,1)}), bf16[4096,512]{1,0:T(8,128)(2,1)}) %all-gather.12.cloned.1.call-update) | async-done | bytes 4194320 | tf_op jit(solution)/shard_map/all_gather | solution.py:144
  131.8 8.5 %fusion.23 = f32[512,512]{1,0:T(8,128)S(1)} fusion(bf16[4096,512]{1,0:T(8,128)(2,1)} %all-gather.12.cloned.1.call-done, bf16[512,4096]{1,0:T(8,128)(2,1)} %bitcast.105, bf16[512,4096]{1,0:T(8,128)(2,1)} %bitcast.112, f32[4096]{0:T(1024)S(1)} %bitcast.127, bf16[5,32,4096]{2,1,0:T(8,128)(2,1)} %param.27, bf16[512,160]{0,1:T(8,128)(2,1)S(1)} %fusion.28), kind=kOutput, calls=%fused_computation.48 | convolution fusion | flops 2296381440 | bytes 13942784 | tf_op jit(solution)/shard_map/dot_general | solution.py:149
  142.2 70.5 %all-gather.14.cloned.1.call-done = bf16[4096,512]{1,0:T(8,128)(2,1)} async-done(((bf16[1024,512]{1,0:T(8,128)(2,1)}), bf16[4096,512]{1,0:T(8,128)(2,1)}) %all-gather.14.cloned.1.call-update) | async-done | bytes 4194320 | tf_op jit(solution)/shard_map/all_gather | solution.py:143
  212.7 8.6 %fusion.22 = f32[512,512]{1,0:T(8,128)S(1)} fusion(bf16[4096,512]{1,0:T(8,128)(2,1)} %all-gather.14.cloned.1.call-done, bf16[512,4096]{1,0:T(8,128)(2,1)} %bitcast.106, bf16[512,4096]{1,0:T(8,128)(2,1)} %bitcast.113, f32[4096]{0:T(1024)S(1)} %bitcast.126, bf16[5,32,4096]{2,1,0:T(8,128)(2,1)} %param.27, bf16[512,160]{0,1:T(8,128)(2,1)S(1)} %fusion.28), kind=kOutput, calls=%fused_computation.47 | convolution fusion | flops 2296381440 | bytes 13942784 | tf_op jit(solution)/shard_map/dot_general | solution.py:149
  223.1 6.9 %fusion.32 = bf16[512,64]{0,1:T(8,128)(2,1)S(1)} fusion(bf16[4096,64]{0,1:T(8,128)(2,1)S(1)} %copy-done.19, bf16[512,4096]{1,0:T(8,128)(2,1)} %bitcast.107, bf16[512,4096]{1,0:T(8,128)(2,1)} %bitcast.114, f32[4096]{0:T(1024)S(1)} %bitcast.125, bf16[5,32,4096]{2,1,0:T(8,128)(2,1)} %param.27, bf16[512,160]{0,1:T(8,128)(2,1)S(1)} %fusion.28), kind=kOutput, calls=%fused_computation.53 | convolution fusion | flops 417366016 | bytes 9289728 | tf_op jit(solution)/shard_map/dot_general | solution.py:154
  234.1 59.4 %all-gather.10.cloned.1.call-done = bf16[4096,512]{1,0:T(8,128)(2,1)} async-done(((bf16[1024,512]{1,0:T(8,128)(2,1)}), bf16[4096,512]{1,0:T(8,128)(2,1)}) %all-gather.10.cloned.1.call-update) | async-done | bytes 4194320 | tf_op jit(solution)/shard_map/all_gather | solution.py:142
  293.4 8.6 %fusion.24 = f32[512,512]{1,0:T(8,128)S(1)} fusion(bf16[4096,512]{1,0:T(8,128)(2,1)} %all-gather.10.cloned.1.call-done, bf16[512,4096]{1,0:T(8,128)(2,1)} %bitcast.108, bf16[512,4096]{1,0:T(8,128)(2,1)} %bitcast.115, f32[4096]{0:T(1024)S(1)} %bitcast.124, bf16[5,32,4096]{2,1,0:T(8,128)(2,1)} %param.27, bf16[512,160]{0,1:T(8,128)(2,1)} %copy-done.25), kind=kOutput, calls=%fused_computation.49 | convolution fusion | flops 2296381440 | bytes 13942784 | tf_op jit(solution)/shard_map/dot_general | solution.py:149
  305.3 2.2 gather_fusion.5
  307.7 6.3 %exponential_multiply_fusion = (f32[32,16,8,64]{3,2,1,0:T(8,128)}, f32[32,16,8,64]{3,2,1,0:T(8,128)}, f32[32,16,8]{2,1,0:T(8,128)S(1)}, f32[32,16,8,64]{3,2,1,0:T(8,128)}) fusion(f32[32,16,8,64]{3,2,1,0:T(8,128)} %mul.159, f32[32,16,8,64]{3,2,1,0:T(8,128)S(1)} %fusion.77, f32[32,8,64]{2,1,0:T(8,128)S(1)} %get-tuple-element.4, ...), kind=kLoop, calls=%fused_computation.35 | loop fusion | flops 1830912 | bytes 6375936 | tf_op jit(solution)/shard_map/mul | solution.py:81
  314.0 15.2 %multiply_reduce_fusion = f32[32,16,16,8]{3,2,1,0:T(8,128)} fusion(f32[32,16,8,64]{3,2,1,0:T(8,128)S(1)} %fusion.77, f32[32,16,8,64]{3,2,1,0:T(8,128)} %get-tuple-element.10, f32[32,16,8,64]{3,2,1,0:T(8,128)} %mul.159, f32[32,16,8,64]{3,2,1,0:T(8,128)} %reshape.354, pred[16,16]{1,0:T(8,128)(4,1)S(1)} %iota_compare_fusion.3), kind=kLoop, calls=%fused_computation.7 | loop fusion | flops 20905984 | bytes 4456704 | tf_op jit(solution)/shard_map/reduce_sum | solution.py:69
  329.3 4.0 copy.69
  333.3 10.2 %fusion.11 = f32[32,8,16,64]{3,2,1,0:T(8,128)S(1)} fusion(f32[32,8,64,64]{3,2,1,0:T(8,128)} %param.23, f32[32,16,8,64]{3,2,1,0:T(8,128)S(1)} %copy-done.6), kind=kOutput, calls=%fused_computation.33 | convolution fusion | flops 201326592 | bytes 6291456 | tf_op jit(solution)/shard_map/bthi,bhij->bthj/dot_general | solution.py:60
  343.5 3.6 fusion.76
  348.9 4.5 copy.82
  354.2 19.7 %multiply_add_fusion = bf16[32,8,64,64]{3,2,1,0:T(8,128)(2,1)} fusion(f32[32,8,64,64]{3,2,1,0:T(8,128)} %param.23, f32[32,8,64]{2,1,0:T(8,128)S(1)} %get-tuple-element.3, f32[32,16,8,64]{3,2,1,0:T(8,128)} %get-tuple-element.7, f32[32,16,8,64]{3,2,1,0:T(8,128)} %reshape.356), kind=kOutput, calls=%fused_computation.23 | convolution fusion | flops 204472320 | bytes 8454144 | tf_op jit(solution)/shard_map/bshi,bshj->bhij/dot_general | solution.py:82
  373.9 7.8 %gather_fusion = bf16[64,8,64,64]{3,2,1,0:T(8,128)(2,1)} fusion(bf16[32,8,64,64]{3,2,1,0:T(8,128)(2,1)} %multiply_add_fusion, s32[1024]{0:T(1024)S(1)} %pad_clamp_fusion.2), kind=kCustom, calls=%fused_computation | custom fusion | bytes 8388864 | tf_op jit(solution)/shard_map/gather | solution.py:218
  383.2 3.5 all-to-all-start.1
  386.7 10.5 %select_convert_fusion = bf16[4,16,8,64,64]{4,3,2,1,0:T(8,128)(2,1)} fusion(bf16[4,16,8,64,64]{4,3,2,1,0:T(8,128)(2,1)} %bitcast.103, pred[4,16]{1,0:T(4,128)(4,1)S(1)} %and_reduce_fusion), kind=kLoop, calls=%fused_computation.15 | loop fusion | flops 2097152 | bytes 8388672 | tf_op jit(solution)/shard_map/convert_element_type | solution.py:225
  397.3 2.2 copy.72
  403.4 9.7 %reshape.439 = bf16[4,2,262144]{2,1,0:T(2,128)(2,1)} reshape(bf16[4,16,8,64,64]{4,3,2,1,0:T(8,128)(2,1)} %select_convert_fusion) | data formatting | bytes 8388608
  413.1 5.1 all-to-all-start
  418.5 9.7 %multiply_convert_fusion = bf16[512,512]{1,0:T(8,128)(2,1)} fusion(bf16[4096,512]{1,0:T(8,128)(2,1)} %all-gather.16.cloned.1.call-done, bf16[512,4096]{1,0:T(8,128)(2,1)} %bitcast.109, bf16[512,4096]{1,0:T(8,128)(2,1)} %bitcast.116, f32[4096]{0:T(1024)S(1)} %bitcast.123, f32[512,512]{1,0:T(8,128)S(1)} %copy-done.12, f32[512,512]{1,0:T(8,128)S(1)} %copy-done.11, ...), kind=kOutput, calls=%fused_computation.57 | convolution fusion | flops 2299002880 | bytes 16568320 | tf_op jit(solution)/shard_map/dot_general | solution.py:149
  428.2 67.7 %all-gather.18.cloned.1.call-done = bf16[512,4096]{1,0:T(8,128)(2,1)} async-done(((bf16[512,1024]{1,0:T(8,128)(2,1)}), bf16[512,4096]{1,0:T(8,128)(2,1)}) %all-gather.18.cloned.1.call-update) | async-done | bytes 4194320 | tf_op jit(solution)/shard_map/all_gather | solution.py:180
  495.9 6.7 %convolution_convert_fusion = bf16[512,4096]{1,0:T(8,128)(2,1)} fusion(bf16[512,512]{1,0:T(8,128)(2,1)} %multiply_convert_fusion, bf16[512,4096]{1,0:T(8,128)(2,1)} %all-gather.18.cloned.1.call-done), kind=kOutput, calls=%fused_computation.24 | convolution fusion | flops 2149580800 | bytes 8912896 | tf_op jit(solution)/shard_map/dot_general | solution.py:182
  505.6 40.1 %all-to-all-done = bf16[4,2,262144]{2,1,0:T(2,128)(2,1)} async-done(((bf16[4,2,262144]{2,1,0:T(2,128)(2,1)}), bf16[4,2,262144]{2,1,0:T(2,128)(2,1)}, u32[]{:S(2)}, u32[]{:S(2)}) %all-to-all-start) | async-done | bytes 4194336 | tf_op jit(solution)/shard_map/all_to_all | solution.py:224
  545.7 9.3 %reshape.440 = bf16[4,16,8,64,64]{4,3,2,1,0:T(8,128)(2,1)} reshape(bf16[4,2,262144]{2,1,0:T(2,128)(2,1)} %all-to-all-done) | data formatting | bytes 8388608
  555.0 11.3 %bitcast_convert_fusion = f32[64,8,64,64]{3,2,1,0:T(8,128)} fusion(bf16[4,16,8,64,64]{4,3,2,1,0:T(8,128)(2,1)} %reshape.440), kind=kLoop, calls=%fused_computation.22 | loop fusion | flops 2097152 | bytes 12582912 | tf_op jit(solution)/shard_map/reshape | solution.py:236
  566.3 10.4 %gather_fusion.2 = f32[32,8,64,64]{3,2,1,0:T(8,128)} fusion(f32[64,8,64,64]{3,2,1,0:T(8,128)} %bitcast_convert_fusion, s32[1024]{0:T(1024)S(1)} %pad_clamp_fusion), kind=kCustom, calls=%fused_computation.2 | custom fusion | bytes 8388736 | tf_op jit(solution)/shard_map/gather | solution.py:236
  576.7 2.1 fusion.34
  (133 shorter events, 31.8 us)
Async XLA Ops:
  7.2 47.9 %copy-start = (bf16[4096,160]{0,1:T(8,128)(2,1)S(1)}, bf16[4096,160]{0,1:T(8,128)(2,1)}, u32[]{:S(2)}) copy-start(bf16[4096,160]{0,1:T(8,128)(2,1)} %param.26) | copy-start | bytes 3932164
  7.2 4.0 copy-start.18
  7.2 4.2 copy-start.24
  7.2 5.0 copy-start.15
  7.2 16.4 %copy-start.14 = (f32[5,4096]{1,0:T(8,128)S(1)}, f32[5,4096]{1,0:T(8,128)}, u32[]{:S(2)}) copy-start(f32[5,4096]{1,0:T(8,128)} %param.25) | copy-start | bytes 245764
  7.2 42.2 %all-gather.8.cloned.1.call-start = ((), (), s32[]{:S(2)}) async-start(), calls=%async_computation.3 | async-start | bytes 4718592 | tf_op jit(solution)/shard_map/all_gather | solution.py:128
  8.0 123.8 %all-gather.12.cloned.1.call-start = ((), (), s32[]{:S(2)}) async-start(), calls=%async_computation.5 | async-start | bytes 5242880 | tf_op jit(solution)/shard_map/all_gather | solution.py:144
  8.7 204.0 %all-gather.14.cloned.1.call-start = ((), (), s32[]{:S(2)}) async-start(), calls=%async_computation.6 | async-start | bytes 5242880 | tf_op jit(solution)/shard_map/all_gather | solution.py:143
  9.4 284.0 %all-gather.10.cloned.1.call-start = ((), (), s32[]{:S(2)}) async-start(), calls=%async_computation.4 | async-start | bytes 5242880 | tf_op jit(solution)/shard_map/all_gather | solution.py:142
  10.0 408.5 %all-gather.16.cloned.1.call-start = ((), (), s32[]{:S(2)}) async-start(), calls=%async_computation.7 | async-start | bytes 5242880 | tf_op jit(solution)/shard_map/all_gather | solution.py:145
  10.6 485.3 %all-gather.18.cloned.1.call-start = ((), (), s32[]{:S(2)}) async-start(), calls=%async_computation.8 | async-start | bytes 5242880 | tf_op jit(solution)/shard_map/all_gather | solution.py:180
  23.1 30.1 %copy-start.8 = (bf16[32,1,4096]{2,0,1:T(8,128)(2,1)}, bf16[32,1,4096]{2,0,1:T(8,128)(2,1)S(1)}, u32[]{:S(2)}) copy-start(bf16[32,1,4096]{2,0,1:T(8,128)(2,1)S(1)} %broadcast_in_dim.75) | copy-start | bytes 786436
  49.4 5.7 copy-start.3
  49.4 5.7 copy-start.20
  57.1 166.0 %copy-start.25 = (bf16[512,160]{0,1:T(8,128)(2,1)}, bf16[512,160]{0,1:T(8,128)(2,1)S(1)}, u32[]{:S(2)}) copy-start(bf16[512,160]{0,1:T(8,128)(2,1)S(1)} %fusion.28) | copy-start | bytes 491524
  212.7 10.4 %copy-start.19 = (bf16[4096,64]{0,1:T(8,128)(2,1)S(1)}, bf16[4096,64]{0,1:T(8,128)(2,1)}, u32[]{:S(2)}) copy-start(bf16[4096,64]{0,1:T(8,128)(2,1)} %param.29) | copy-start | bytes 1572868
  223.1 6.9 %copy-start.13 = (bf16[64,512]{1,0:T(8,128)(2,1)S(1)}, bf16[64,512]{1,0:T(8,128)(2,1)}, u32[]{:S(2)}) copy-start(bf16[64,512]{1,0:T(8,128)(2,1)} %param.30) | copy-start | bytes 196612
  223.1 6.9 %copy-start.17 = (f32[512]{0:T(512)S(1)}, f32[512]{0:T(512)}, u32[]{:S(2)}) copy-start(f32[512]{0:T(512)} %param.28) | copy-start | bytes 6148
  302.0 5.6 copy-start.16
  329.3 4.0 copy-start.6
  333.3 10.2 %copy-start.2 = (f32[32,16,8,64]{3,2,1,0:T(8,128)S(1)}, f32[32,16,8,64]{3,2,1,0:T(8,128)}, u32[]{:S(2)}) copy-start(f32[32,16,8,64]{3,2,1,0:T(8,128)} %reshape.356) | copy-start | bytes 3145732
  333.3 10.2 %copy-start.5 = (f32[32,16,16,8]{2,1,3,0:T(8,128)S(1)}, f32[32,16,16,8]{2,1,3,0:T(8,128)}, u32[]{:S(2)}) copy-start(f32[32,16,16,8]{2,1,3,0:T(8,128)} %copy.69) | copy-start | bytes 786436
  348.8 4.5 copy-start.9
  383.2 29.9 %all-to-all-start.1 = ((bf16[4,16,512]{2,1,0:T(8,128)(2,1)}), bf16[4,16,512]{2,1,0:T(8,128)(2,1)S(1)}, u32[]{:S(2)}, u32[]{:S(2)}) async-start(bf16[4,16,512]{2,1,0:T(8,128)(2,1)} %fusion.56), calls=%async_computation.2 | async-start | bytes 131072 | tf_op jit(solution)/shard_map/all_to_all | solution.py:227
  413.1 5.4 copy-start.11
  413.1 5.4 copy-start.12
  413.1 5.5 copy-start.21
  413.1 5.5 copy-start.22
  413.1 132.6 %all-to-all-start = ((bf16[4,2,262144]{2,1,0:T(2,128)(2,1)}), bf16[4,2,262144]{2,1,0:T(2,128)(2,1)}, u32[]{:S(2)}, u32[]{:S(2)}) async-start(bf16[4,2,262144]{2,1,0:T(2,128)(2,1)} %reshape.439), calls=%async_computation.1 | async-start | bytes 8388608 | tf_op jit(solution)/shard_map/all_to_all | solution.py:224
  418.2 158.5 %reduce-scatter.2.cloned.1.call-start = ((), (), s32[]{:S(2)}) async-start(), calls=%async_computation.9 | async-start | bytes 4718592 | tf_op jit(solution)/shard_map/reduce_scatter | solution.py:181
  566.3 10.4 %copy-start.10 = (bf16[4,16,4096]{2,1,0:T(8,128)(2,1)S(1)}, bf16[4,16,4096]{2,1,0:T(8,128)(2,1)}, u32[]{:S(2)}) copy-start(bf16[4,16,4096]{2,1,0:T(8,128)(2,1)} %param.21) | copy-start | bytes 1572868
  566.3 12.5 %copy-start.1 = (bf16[4096,160]{0,1:T(8,128)(2,1)S(1)}, bf16[4096,160]{0,1:T(8,128)(2,1)}, u32[]{:S(2)}) copy-start(bf16[4096,160]{0,1:T(8,128)(2,1)} %param.26) | copy-start | bytes 3932164
  (3 other events, 4.5 us)
Sparse Core Ops, SparseCore 0:
  9.9 39.4 all-gather.7
  51.0 80.7 all-gather.11
  133.4 79.2 all-gather.13
  214.1 79.2 all-gather.9
  294.9 79.2 all-gather.15
  375.6 120.2 all-gather.17
  502.8 49.4 reduce-scatter.1
where the time goes:
time: 590 us; the launch traced here: 586 us
  waiting for transfers between devices  342 us (58%)
  matrix products  84.8 us (14%)
  local copies, waits for them, and re-layouts  70.2 us (12%)
  other arithmetic  54.3 us (9%)
  between operations  15 us (3%)
  blocking collectives  10.8 us (2%)
  starting transfers between devices  9.1 us (2%)
    all_gather x1, waiting for transfers between devices, on_device(): lax.all_gather(payload_matrix, 'dp', axis=0, tiled=True)  74.7 us
    all_gather x1, waiting for transfers between devices, on_device(): lax.all_gather(lookup_matrix, 'dp', axis=0, tiled=True)  70.5 us
    all_gather x1, waiting for transfers between devices, on_device(): out_cols = lax.all_gather(emission_matrix, 'dp', axis=1, tiled=True)  67.7 us
    all_gather x1, waiting for transfers between devices, on_device(): lax.all_gather(acceptor_matrix, 'dp', axis=0, tiled=True)  59.4 us
    all_to_all x1, waiting for transfers between devices, on_device(): lax.all_to_all(send_state.astype(jnp.bfloat16), 'dp', split_axis=0, conca...  40.1 us
    dot_general x4, matrix products, on_device(): jnp.dot(source_rows, piece, preferred_element_type=jnp.float32)  35.4 us
    all_gather x1, waiting for transfers between devices, on_device(): lax.all_gather(guess_vectors, 'mp', axis=0, tiled=True)  25.6 us
    unnamed x55, local copies, waits for them, and re-layouts  21.5 us
  transfers between devices with their start and end apart: 9, of which 6 were waited for; matrix products, arithmetic and copies ran while one was open for 35% of the time, Pallas kernels for 0%

commit v1 on v0

--- a/solution.py
+++ b/solution.py
@@ -5,6 +5,22 @@
 
 GROUP_DIMENSION = 64
 norm_eps = 0.00064
+
+
+def gather_around(x, axis, dim):
+    ways, here, step = (lax.axis_size(axis), lax.axis_index(axis), x.shape[dim])
+    shape = [n * ways if d == dim else n for d, n in enumerate(x.shape)]
+    full = lax.dynamic_update_slice_in_dim(jnp.zeros(shape, x.dtype), x, here * step, axis=dim)
+    going_up = going_down = x
+    for far in range(1, ways // 2 + 1):
+        going_up = lax.ppermute(going_up, axis, [(d, (d + 1) % ways) for d in range(ways)])
+        full = lax.dynamic_update_slice_in_dim(full, going_up, (here - far) % ways * step, axis=dim)
+        if 2 * far < ways:
+            going_down = lax.ppermute(going_down, axis, [(d, (d - 1) % ways) for d in range(ways)])
+            full = lax.dynamic_update_slice_in_dim(
+                full, going_down, (here + far) % ways * step, axis=dim
+            )
+    return full
 
 
 def token_mixes(
@@ -140,7 +156,7 @@
     sources = (shift_mixed_rows[3], shift_mixed_rows[1], shift_mixed_rows[2], shift_mixed_rows[4])
     pieces = (
         lax.all_gather(acceptor_matrix, "dp", axis=0, tiled=True),
-        lax.all_gather(lookup_matrix, "dp", axis=0, tiled=True),
+        gather_around(lookup_matrix, "dp", 0),
         lax.all_gather(payload_matrix, "dp", axis=0, tiled=True),
         lax.all_gather(gating_matrix, "dp", axis=0, tiled=True),
     )

time: 590 us -> 530 us (0.90)
  waiting for transfers between devices: 342 us -> 267 us
  local copies, waits for them, and re-layouts: 70.2 us -> 79.3 us
    all_gather x1 -> x0, waiting for transfers between devices: 70.5 us -> none  [on_device(): lax.all_gather(lookup_matrix, 'dp', axis=0, tiled=True)]
    ppermute x0 -> x3, waiting for transfers between devices: none -> 69.6 us  [the longest x2 50.7 us: gather_around(): lax.ppermute(going_up, axis, [(d, (d + 1) % ways) for d in range(ways)])]
    all_gather x1, waiting for transfers between devices: 74.7 us -> 37.9 us  [on_device(): lax.all_gather(payload_matrix, 'dp', axis=0, tiled=True)]
    all_gather x1, waiting for transfers between devices: 25.6 us -> 0.01 us  [on_device(): lax.all_gather(guess_vectors, 'mp', axis=0, tiled=True)]
    all_gather x1, waiting for transfers between devices: 59.4 us -> 49.8 us  [on_device(): lax.all_gather(acceptor_matrix, 'dp', axis=0, tiled=True)]
    dynamic_update_slice x0 -> x4, local copies, waits for them, and re-layouts: none -> 6.71 us  [the longest x2 3.31 us: gather_around(): lax.dynamic_update_slice_in_dim(full, going_up, (here - far) % ways * ste...]
    unnamed x55 -> x59, local copies, waits for them, and re-layouts: 21.5 us -> 21.6 us
  transfers between devices with their start and end apart: 9 -> 11, of which waited for: 6 -> 7; matrix products, arithmetic and copies ran while one was open for 35% -> 41% of each run, Pallas kernels for 0% -> 0%
where the time goes in v1:
time: 530 us; the launch traced here: 526 us
  waiting for transfers between devices  267 us (50%)
  matrix products  84.8 us (16%)
  local copies, waits for them, and re-layouts  79.3 us (15%)
  other arithmetic  54.4 us (10%)
  between operations  14.9 us (3%)
  starting transfers between devices  14.2 us (3%)
  blocking collectives  10.4 us (2%)
    all_gather x1, waiting for transfers between devices, on_device(): out_cols = lax.all_gather(emission_matrix, 'dp', axis=1, tiled=True)  67.2 us
    ppermute x2, waiting for transfers between devices, gather_around(): lax.ppermute(going_up, axis, [(d, (d + 1) % ways) for d in range(ways)])  50.7 us
    all_gather x1, waiting for transfers between devices, on_device(): lax.all_gather(acceptor_matrix, 'dp', axis=0, tiled=True)  49.8 us
    all_to_all x1, waiting for transfers between devices, on_device(): lax.all_to_all(send_state.astype(jnp.bfloat16), 'dp', split_axis=0, conca...  40.3 us
    all_gather x1, waiting for transfers between devices, on_device(): lax.all_gather(payload_matrix, 'dp', axis=0, tiled=True)  37.9 us
    dot_general x4, matrix products, on_device(): jnp.dot(source_rows, piece, preferred_element_type=jnp.float32)  35.3 us
    unnamed x59, local copies, waits for them, and re-layouts  21.6 us
    dot_general x1, matrix products, wkv_blocks(): jnp.einsum('bshi,bshj->bhij', weighted, payload_vectors, precision=lax.Pr...  19.8 us
  transfers between devices with their start and end apart: 11, of which 7 were waited for; matrix products, arithmetic and copies ran while one was open for 41% of the time, Pallas kernels for 0%

profile of v1, /device:TPU:0, one launch (start us, length us, event | category | flops | bytes accessed | tf_op | source)
XLA Modules:
  0.0 525.5 jit_solution(11967678795542508828)
XLA Ops:
  10.1 3.1 collective-permute-start
  19.8 10.4 %all-gather = bf16[8,4,4096]{2,1,0:T(4,128)(2,1)S(1)} all-gather(bf16[1,4,4096]{2,1,0:T(4,128)(2,1)S(1)} %bitcast.122), channel_id=1, replica_groups=mesh['dp'=4,'mp'=8] {'mp'}, dimensions={0}, use_global_device_ids=true | all-gather | bytes 294912 | tf_op jit(solution)/shard_map/all_gather | solution.py:145
  30.9 8.7 %collective-permute-done = bf16[1024,512]{1,0:T(8,128)(2,1)} collective-permute-done((bf16[1024,512]{1,0:T(8,128)(2,1)}, bf16[1024,512]{1,0:T(8,128)(2,1)}, u32[]{:S(2)}, u32[]{:S(2)}) %collective-permute-start) | collective-permute-done | bytes 1048608 | tf_op jit(solution)/shard_map/ppermute | solution.py:16
  41.9 18.9 %collective-permute-done.1 = bf16[1024,512]{1,0:T(8,128)(2,1)} collective-permute-done((bf16[1024,512]{1,0:T(8,128)(2,1)}, bf16[1024,512]{1,0:T(8,128)(2,1)}, u32[]{:S(2)}, u32[]{:S(2)}) %collective-permute-start.1) | collective-permute-done | bytes 1048608 | tf_op jit(solution)/shard_map/ppermute | solution.py:19
  60.8 2.4 constant_dynamic-update-slice_fusion.1
  63.1 42.0 %collective-permute-done.2 = bf16[1024,512]{1,0:T(8,128)(2,1)S(1)} collective-permute-done((bf16[1024,512]{1,0:T(8,128)(2,1)}, bf16[1024,512]{1,0:T(8,128)(2,1)S(1)}, u32[]{:S(2)}, u32[]{:S(2)}) %collective-permute-start.2) | collective-permute-done | bytes 1048608 | tf_op jit(solution)/shard_map/ppermute | solution.py:16
  106.2 3.6 pad_maximum_fusion
  113.8 37.9 %all-gather.11.cloned.1.call-done = bf16[4096,512]{1,0:T(8,128)(2,1)} async-done(((bf16[1024,512]{1,0:T(8,128)(2,1)}), bf16[4096,512]{1,0:T(8,128)(2,1)}) %all-gather.11.cloned.1.call-update) | async-done | bytes 4194320 | tf_op jit(solution)/shard_map/all_gather | solution.py:160
  151.7 8.5 %fusion.23 = f32[512,512]{1,0:T(8,128)S(1)} fusion(bf16[4096,512]{1,0:T(8,128)(2,1)} %all-gather.11.cloned.1.call-done, bf16[512,4096]{1,0:T(8,128)(2,1)} %bitcast.105, bf16[512,4096]{1,0:T(8,128)(2,1)} %bitcast.112, f32[4096]{0:T(1024)S(1)} %bitcast.127, bf16[5,32,4096]{2,1,0:T(8,128)(2,1)S(1)} %copy-done.20, bf16[512,160]{0,1:T(8,128)(2,1)S(1)} %fusion.28), kind=kOutput, calls=%fused_computation.48 | convolution fusion | flops 2296381440 | bytes 13942784 | tf_op jit(solution)/shard_map/dot_general | solution.py:165
  161.9 8.6 %fusion.22 = f32[512,512]{1,0:T(8,128)S(1)} fusion(bf16[4096,512]{1,0:T(8,128)(2,1)} %constant_dynamic-update-slice_fusion, bf16[512,4096]{1,0:T(8,128)(2,1)} %bitcast.106, bf16[512,4096]{1,0:T(8,128)(2,1)} %bitcast.113, f32[4096]{0:T(1024)S(1)} %bitcast.126, bf16[5,32,4096]{2,1,0:T(8,128)(2,1)S(1)} %copy-done.20, bf16[512,160]{0,1:T(8,128)(2,1)} %copy-done.27), kind=kOutput, calls=%fused_computation.47 | convolution fusion | flops 2296381440 | bytes 13942784 | tf_op jit(solution)/shard_map/dot_general | solution.py:165
  172.4 6.9 %fusion.32 = bf16[512,64]{0,1:T(8,128)(2,1)S(1)} fusion(bf16[4096,64]{0,1:T(8,128)(2,1)S(1)} %copy-done.21, bf16[512,4096]{1,0:T(8,128)(2,1)} %bitcast.107, bf16[512,4096]{1,0:T(8,128)(2,1)} %bitcast.114, f32[4096]{0:T(1024)S(1)} %bitcast.125, bf16[5,32,4096]{2,1,0:T(8,128)(2,1)S(1)} %copy-done.20, bf16[512,160]{0,1:T(8,128)(2,1)} %copy-done.27), kind=kOutput, calls=%fused_computation.53 | convolution fusion | flops 417366016 | bytes 9289728 | tf_op jit(solution)/shard_map/dot_general | solution.py:170
  183.3 49.8 %all-gather.9.cloned.1.call-done = bf16[4096,512]{1,0:T(8,128)(2,1)} async-done(((bf16[1024,512]{1,0:T(8,128)(2,1)}), bf16[4096,512]{1,0:T(8,128)(2,1)}) %all-gather.9.cloned.1.call-update) | async-done | bytes 4194320 | tf_op jit(solution)/shard_map/all_gather | solution.py:158
  233.1 8.6 %fusion.24 = f32[512,512]{1,0:T(8,128)S(1)} fusion(bf16[4096,512]{1,0:T(8,128)(2,1)} %all-gather.9.cloned.1.call-done, bf16[512,4096]{1,0:T(8,128)(2,1)} %bitcast.108, bf16[512,4096]{1,0:T(8,128)(2,1)} %bitcast.115, f32[4096]{0:T(1024)S(1)} %bitcast.124, bf16[5,32,4096]{2,1,0:T(8,128)(2,1)} %param.27, bf16[512,160]{0,1:T(8,128)(2,1)} %copy-done.27), kind=kOutput, calls=%fused_computation.49 | convolution fusion | flops 2296381440 | bytes 13942784 | tf_op jit(solution)/shard_map/dot_general | solution.py:165
  247.3 6.3 %exponential_multiply_fusion = (f32[32,16,8,64]{3,2,1,0:T(8,128)}, f32[32,16,8,64]{3,2,1,0:T(8,128)}, f32[32,16,8]{2,1,0:T(8,128)S(1)}, f32[32,16,8,64]{3,2,1,0:T(8,128)}) fusion(f32[32,16,8,64]{3,2,1,0:T(8,128)} %mul.175, f32[32,16,8,64]{3,2,1,0:T(8,128)S(1)} %fusion.77, f32[32,8,64]{2,1,0:T(8,128)S(1)} %get-tuple-element.4, ...), kind=kLoop, calls=%fused_computation.35 | loop fusion | flops 1830912 | bytes 6375936 | tf_op jit(solution)/shard_map/mul | solution.py:97
  253.8 15.2 %multiply_reduce_fusion = f32[32,16,16,8]{3,2,1,0:T(8,128)} fusion(f32[32,16,8,64]{3,2,1,0:T(8,128)S(1)} %fusion.77, f32[32,16,8,64]{3,2,1,0:T(8,128)} %get-tuple-element.10, f32[32,16,8,64]{3,2,1,0:T(8,128)} %mul.175, f32[32,16,8,64]{3,2,1,0:T(8,128)} %reshape.354, pred[16,16]{1,0:T(8,128)(4,1)S(1)} %iota_compare_fusion.3), kind=kLoop, calls=%fused_computation.7 | loop fusion | flops 20905984 | bytes 4456704 | tf_op jit(solution)/shard_map/reduce_sum | solution.py:85
  269.0 4.1 copy.69
  273.1 10.2 %fusion.11 = f32[32,8,16,64]{3,2,1,0:T(8,128)S(1)} fusion(f32[32,8,64,64]{3,2,1,0:T(8,128)} %param.23, f32[32,16,8,64]{3,2,1,0:T(8,128)S(1)} %copy-done.6), kind=kOutput, calls=%fused_computation.33 | convolution fusion | flops 201326592 | bytes 6291456 | tf_op jit(solution)/shard_map/bthi,bhij->bthj/dot_general | solution.py:76
  283.3 3.6 fusion.76
  288.7 4.5 copy.82
  294.0 19.8 %multiply_add_fusion = bf16[32,8,64,64]{3,2,1,0:T(8,128)(2,1)} fusion(f32[32,8,64,64]{3,2,1,0:T(8,128)} %param.23, f32[32,8,64]{2,1,0:T(8,128)S(1)} %get-tuple-element.3, f32[32,16,8,64]{3,2,1,0:T(8,128)} %get-tuple-element.7, f32[32,16,8,64]{3,2,1,0:T(8,128)} %reshape.356), kind=kOutput, calls=%fused_computation.23 | convolution fusion | flops 204472320 | bytes 8454144 | tf_op jit(solution)/shard_map/bshi,bshj->bhij/dot_general | solution.py:98
  313.8 7.8 %gather_fusion = bf16[64,8,64,64]{3,2,1,0:T(8,128)(2,1)} fusion(bf16[32,8,64,64]{3,2,1,0:T(8,128)(2,1)} %multiply_add_fusion, s32[1024]{0:T(1024)S(1)} %pad_clamp_fusion.2), kind=kCustom, calls=%fused_computation | custom fusion | bytes 8388864 | tf_op jit(solution)/shard_map/gather | solution.py:234
  323.1 3.5 all-to-all-start.1
  326.6 10.6 %select_convert_fusion = bf16[4,16,8,64,64]{4,3,2,1,0:T(8,128)(2,1)} fusion(bf16[4,16,8,64,64]{4,3,2,1,0:T(8,128)(2,1)} %bitcast.103, pred[4,16]{1,0:T(4,128)(4,1)S(1)} %and_reduce_fusion), kind=kLoop, calls=%fused_computation.15 | loop fusion | flops 2097152 | bytes 8388672 | tf_op jit(solution)/shard_map/convert_element_type | solution.py:241
  343.3 9.7 %reshape.439 = bf16[4,2,262144]{2,1,0:T(2,128)(2,1)} reshape(bf16[4,16,8,64,64]{4,3,2,1,0:T(8,128)(2,1)} %select_convert_fusion) | data formatting | bytes 8388608
  353.0 5.1 all-to-all-start
  358.4 9.7 %multiply_convert_fusion = bf16[512,512]{1,0:T(8,128)(2,1)} fusion(bf16[4096,512]{1,0:T(8,128)(2,1)} %all-gather.13.cloned.1.call-done, bf16[512,4096]{1,0:T(8,128)(2,1)} %bitcast.109, bf16[512,4096]{1,0:T(8,128)(2,1)} %bitcast.116, f32[4096]{0:T(1024)S(1)} %bitcast.123, f32[512,512]{1,0:T(8,128)S(1)} %copy-done.13, f32[512,512]{1,0:T(8,128)S(1)} %copy-done.11, ...), kind=kOutput, calls=%fused_computation.57 | convolution fusion | flops 2299002880 | bytes 16568320 | tf_op jit(solution)/shard_map/dot_general | solution.py:165
  368.1 67.2 %all-gather.15.cloned.1.call-done = bf16[512,4096]{1,0:T(8,128)(2,1)} async-done(((bf16[512,1024]{1,0:T(8,128)(2,1)}), bf16[512,4096]{1,0:T(8,128)(2,1)}) %all-gather.15.cloned.1.call-update) | async-done | bytes 4194320 | tf_op jit(solution)/shard_map/all_gather | solution.py:196
  435.4 6.6 %convolution_convert_fusion = bf16[512,4096]{1,0:T(8,128)(2,1)} fusion(bf16[512,512]{1,0:T(8,128)(2,1)} %multiply_convert_fusion, bf16[512,4096]{1,0:T(8,128)(2,1)} %all-gather.15.cloned.1.call-done), kind=kOutput, calls=%fused_computation.24 | convolution fusion | flops 2149580800 | bytes 8912896 | tf_op jit(solution)/shard_map/dot_general | solution.py:198
  445.0 40.3 %all-to-all-done = bf16[4,2,262144]{2,1,0:T(2,128)(2,1)} async-done(((bf16[4,2,262144]{2,1,0:T(2,128)(2,1)}), bf16[4,2,262144]{2,1,0:T(2,128)(2,1)}, u32[]{:S(2)}, u32[]{:S(2)}) %all-to-all-start) | async-done | bytes 4194336 | tf_op jit(solution)/shard_map/all_to_all | solution.py:240
  485.3 9.3 %reshape.440 = bf16[4,16,8,64,64]{4,3,2,1,0:T(8,128)(2,1)} reshape(bf16[4,2,262144]{2,1,0:T(2,128)(2,1)} %all-to-all-done) | data formatting | bytes 8388608
  494.6 11.3 %bitcast_convert_fusion = f32[64,8,64,64]{3,2,1,0:T(8,128)} fusion(bf16[4,16,8,64,64]{4,3,2,1,0:T(8,128)(2,1)} %reshape.440), kind=kLoop, calls=%fused_computation.22 | loop fusion | flops 2097152 | bytes 12582912 | tf_op jit(solution)/shard_map/reshape | solution.py:252
  506.0 10.4 %gather_fusion.2 = f32[32,8,64,64]{3,2,1,0:T(8,128)} fusion(f32[64,8,64,64]{3,2,1,0:T(8,128)} %bitcast_convert_fusion, s32[1024]{0:T(1024)S(1)} %pad_clamp_fusion), kind=kCustom, calls=%fused_computation.2 | custom fusion | bytes 8388736 | tf_op jit(solution)/shard_map/gather | solution.py:252
  (145 shorter events, 45.9 us)
Async XLA Ops:
  7.2 104.6 %copy-start = (bf16[4096,160]{0,1:T(8,128)(2,1)S(1)}, bf16[4096,160]{0,1:T(8,128)(2,1)}, u32[]{:S(2)}) copy-start(bf16[4096,160]{0,1:T(8,128)(2,1)} %param.26) | copy-start | bytes 3932164
  7.2 8.1 %copy-start.19 = (s32[128]{0:T(128)S(1)}, s32[128]{0:T(128)}, u32[]{:S(2)}) copy-start(s32[128]{0:T(128)} %param.40) | copy-start | bytes 1540
  7.2 8.2 %copy-start.26 = (s32[128]{0:T(128)S(1)}, s32[128]{0:T(128)}, u32[]{:S(2)}) copy-start(s32[128]{0:T(128)} %param.41) | copy-start | bytes 1540
  7.2 99.0 %all-gather.7.cloned.1.call-start = ((), (), s32[]{:S(2)}) async-start(), calls=%async_computation.3 | async-start | bytes 4718592 | tf_op jit(solution)/shard_map/all_gather | solution.py:144
  7.9 10.7 %copy-start.12 = (bf16[1024,512]{1,0:T(8,128)(2,1)S(1)}, bf16[1024,512]{1,0:T(8,128)(2,1)}, u32[]{:S(2)}) copy-start(bf16[1024,512]{1,0:T(8,128)(2,1)} %param.33) | copy-start | bytes 3145732
  7.9 143.7 %all-gather.11.cloned.1.call-start = ((), (), s32[]{:S(2)}) async-start(), calls=%async_computation.5 | async-start | bytes 5242880 | tf_op jit(solution)/shard_map/all_gather | solution.py:160
  8.7 224.4 %all-gather.9.cloned.1.call-start = ((), (), s32[]{:S(2)}) async-start(), calls=%async_computation.4 | async-start | bytes 5242880 | tf_op jit(solution)/shard_map/all_gather | solution.py:158
  9.4 10.3 %copy-start.16 = (bf16[4,4096]{1,0:T(4,128)(2,1)S(1)}, bf16[4,4096]{1,0:T(4,128)(2,1)}, u32[]{:S(2)}) copy-start(bf16[4,4096]{1,0:T(4,128)(2,1)} %param.22) | copy-start | bytes 98308
  9.4 349.0 %all-gather.13.cloned.1.call-start = ((), (), s32[]{:S(2)}) async-start(), calls=%async_computation.6 | async-start | bytes 5242880 | tf_op jit(solution)/shard_map/all_gather | solution.py:161
  10.0 425.4 %all-gather.15.cloned.1.call-start = ((), (), s32[]{:S(2)}) async-start(), calls=%async_computation.7 | async-start | bytes 5242880 | tf_op jit(solution)/shard_map/all_gather | solution.py:196
  10.1 29.5 %collective-permute-start = (bf16[1024,512]{1,0:T(8,128)(2,1)}, bf16[1024,512]{1,0:T(8,128)(2,1)}, u32[]{:S(2)}, u32[]{:S(2)}) collective-permute-start(bf16[1024,512]{1,0:T(8,128)(2,1)} %param.33), channel_id=1, source_target_pairs={{0,8},{8,16},{16,24},{24,0},{1,9},{9,17},{17,25},{25,1},{2,10},{10... | collective-permute-start | bytes 3145736 | tf_op jit(solution)/shard_map/ppermute | solution.py:16
  13.1 47.6 %collective-permute-start.1 = (bf16[1024,512]{1,0:T(8,128)(2,1)}, bf16[1024,512]{1,0:T(8,128)(2,1)}, u32[]{:S(2)}, u32[]{:S(2)}) collective-permute-start(bf16[1024,512]{1,0:T(8,128)(2,1)} %param.33), channel_id=1, source_target_pairs={{0,24},{8,0},{16,8},{24,16},{1,25},{9,1},{17,9},{25,17},{2,26},{10... | collective-permute-start | bytes 3145736 | tf_op jit(solution)/shard_map/ppermute | solution.py:19
  15.3 24.3 %copy-start.15 = (f32[5,4096]{1,0:T(8,128)S(1)}, f32[5,4096]{1,0:T(8,128)}, u32[]{:S(2)}) copy-start(f32[5,4096]{1,0:T(8,128)} %param.25) | copy-start | bytes 245764
  30.3 79.6 %copy-start.8 = (bf16[32,1,4096]{2,0,1:T(8,128)(2,1)}, bf16[32,1,4096]{2,0,1:T(8,128)(2,1)S(1)}, u32[]{:S(2)}) copy-start(bf16[32,1,4096]{2,0,1:T(8,128)(2,1)S(1)} %broadcast_in_dim.77) | copy-start | bytes 786436
  39.5 65.6 %collective-permute-start.2 = (bf16[1024,512]{1,0:T(8,128)(2,1)}, bf16[1024,512]{1,0:T(8,128)(2,1)S(1)}, u32[]{:S(2)}, u32[]{:S(2)}) collective-permute-start(bf16[1024,512]{1,0:T(8,128)(2,1)} %collective-permute-done), channel_id=1, source_target_pairs={{0,8},{8,16},{16,24},{24,0},{1,9},{9,17},{17,25},{25,1},{2,10},{10... | collective-permute-start | bytes 3145736 | tf_op jit(solution)/shard_map/ppermute | solution.py:16
  106.2 5.6 %copy-start.3 = (bf16[32,16,4096]{2,1,0:T(8,128)(2,1)S(1)}, bf16[32,16,4096]{2,1,0:T(8,128)(2,1)}, u32[]{:S(2)}) copy-start(bf16[32,16,4096]{2,1,0:T(8,128)(2,1)} %all-gather.7.cloned.1.call-done) | copy-start | bytes 12582916
  106.2 5.6 %copy-start.22 = (f32[4096]{0:T(1024)S(1)}, f32[4096]{0:T(1024)}, u32[]{:S(2)}) copy-start(f32[4096]{0:T(1024)} %param.24) | copy-start | bytes 49156
  111.8 39.9 %copy-start.20 = (bf16[5,32,4096]{2,1,0:T(8,128)(2,1)S(1)}, bf16[5,32,4096]{2,1,0:T(8,128)(2,1)}, u32[]{:S(2)}) copy-start(bf16[5,32,4096]{2,1,0:T(8,128)(2,1)} %param.27) | copy-start | bytes 3932164
  113.8 46.3 %copy-start.27 = (bf16[512,160]{0,1:T(8,128)(2,1)}, bf16[512,160]{0,1:T(8,128)(2,1)S(1)}, u32[]{:S(2)}) copy-start(bf16[512,160]{0,1:T(8,128)(2,1)S(1)} %fusion.28) | copy-start | bytes 491524
  161.9 10.5 %copy-start.21 = (bf16[4096,64]{0,1:T(8,128)(2,1)S(1)}, bf16[4096,64]{0,1:T(8,128)(2,1)}, u32[]{:S(2)}) copy-start(bf16[4096,64]{0,1:T(8,128)(2,1)} %param.29) | copy-start | bytes 1572868
  172.3 6.9 %copy-start.14 = (bf16[64,512]{1,0:T(8,128)(2,1)S(1)}, bf16[64,512]{1,0:T(8,128)(2,1)}, u32[]{:S(2)}) copy-start(bf16[64,512]{1,0:T(8,128)(2,1)} %param.30) | copy-start | bytes 196612
  172.3 6.9 %copy-start.18 = (f32[512]{0:T(512)S(1)}, f32[512]{0:T(512)}, u32[]{:S(2)}) copy-start(f32[512]{0:T(512)} %param.28) | copy-start | bytes 6148
  241.6 5.7 %copy-start.17 = (f32[8,64]{1,0:T(8,128)S(1)}, f32[8,64]{1,0:T(8,128)}, u32[]{:S(2)}) copy-start(f32[8,64]{1,0:T(8,128)} %param.31) | copy-start | bytes 6148
  273.1 10.2 %copy-start.2 = (f32[32,16,8,64]{3,2,1,0:T(8,128)S(1)}, f32[32,16,8,64]{3,2,1,0:T(8,128)}, u32[]{:S(2)}) copy-start(f32[32,16,8,64]{3,2,1,0:T(8,128)} %reshape.356) | copy-start | bytes 3145732
  273.1 10.2 %copy-start.5 = (f32[32,16,16,8]{2,1,3,0:T(8,128)S(1)}, f32[32,16,16,8]{2,1,3,0:T(8,128)}, u32[]{:S(2)}) copy-start(f32[32,16,16,8]{2,1,3,0:T(8,128)} %copy.69) | copy-start | bytes 786436
  323.1 29.9 %all-to-all-start.1 = ((bf16[4,16,512]{2,1,0:T(8,128)(2,1)}), bf16[4,16,512]{2,1,0:T(8,128)(2,1)S(1)}, u32[]{:S(2)}, u32[]{:S(2)}) async-start(bf16[4,16,512]{2,1,0:T(8,128)(2,1)} %fusion.56), calls=%async_computation.2 | async-start | bytes 131072 | tf_op jit(solution)/shard_map/all_to_all | solution.py:243
  353.0 5.4 %copy-start.23 = (f32[512]{0:T(512)S(1)}, f32[512]{0:T(512)}, u32[]{:S(2)}) copy-start(f32[512]{0:T(512)} %param.38) | copy-start | bytes 6148
  353.0 5.5 %copy-start.24 = (f32[512]{0:T(512)S(1)}, f32[512]{0:T(512)}, u32[]{:S(2)}) copy-start(f32[512]{0:T(512)} %param.37) | copy-start | bytes 6148
  353.0 132.3 %all-to-all-start = ((bf16[4,2,262144]{2,1,0:T(2,128)(2,1)}), bf16[4,2,262144]{2,1,0:T(2,128)(2,1)}, u32[]{:S(2)}, u32[]{:S(2)}) async-start(bf16[4,2,262144]{2,1,0:T(2,128)(2,1)} %reshape.439), calls=%async_computation.1 | async-start | bytes 8388608 | tf_op jit(solution)/shard_map/all_to_all | solution.py:240
  358.1 158.2 %reduce-scatter.2.cloned.1.call-start = ((), (), s32[]{:S(2)}) async-start(), calls=%async_computation.8 | async-start | bytes 4718592 | tf_op jit(solution)/shard_map/reduce_scatter | solution.py:197
  506.0 10.4 %copy-start.10 = (bf16[4,16,4096]{2,1,0:T(8,128)(2,1)S(1)}, bf16[4,16,4096]{2,1,0:T(8,128)(2,1)}, u32[]{:S(2)}) copy-start(bf16[4,16,4096]{2,1,0:T(8,128)(2,1)} %param.21) | copy-start | bytes 1572868
  506.0 12.5 %copy-start.1 = (bf16[4096,160]{0,1:T(8,128)(2,1)S(1)}, bf16[4096,160]{0,1:T(8,128)(2,1)}, u32[]{:S(2)}) copy-start(bf16[4096,160]{0,1:T(8,128)(2,1)} %param.26) | copy-start | bytes 3932164
  (7 other events, 23.9 us)
Sparse Core Ops, SparseCore 0:
  9.9 40.2 all-gather.6
  51.8 99.7 all-gather.10
  153.2 79.7 all-gather.8
  234.5 79.2 all-gather.12
  315.2 120.1 all-gather.14
  442.2 49.4 reduce-scatter.1
